TPU v7x, 32 devices: a whole 2x2x4 slice. The times are simulated.
32 devices in a mesh: patch: 4 (over y, x), sub: 8 (over z, core).
Axes of the slice: x: 2, y: 2, z: 4, core: 2. Of those that a mesh axis runs over, the one named last changes fastest.
Arguments:
- element_temps: float32 [16384, 64], P(('patch', 'sub')), may hold values from -6 to 6
- quad_weights: float32 [16384, 64], P(('patch', 'sub')), may hold values from 0.3 to 3
- basis_values: float32 [64, 64], replicated, may hold values from -0.75 to 0.75
- basis_grads: float32 [3, 64, 64], replicated, may hold values from -0.75 to 0.75
- owner_block: int32 [16384, 1], P(('patch', 'sub')), may hold values from 0 to 63; in each aligned block of 512 rows (0 to 511, 512 to 1023, ...) at most 16 rows name the same one
- column_ref: int32 [16384, 1], P(('patch', 'sub')), may hold values from 0 to 31
- quadrant: int32 [16384, 1], P(('patch', 'sub')), may hold values from 0 to 3
- active_counts: int32 [32], P(('patch', 'sub')), may hold values from 256 to 512, as said below
- send_list: int32 [256, 2], P(('patch', 'sub')), may hold values from 0 to 7
- iface_list: int32 [64, 4], P(('patch', 'sub')), may hold values from 0 to 7
- newton_residual: float32 [256, 128], P(('patch', 'sub')), may hold values from -6 to 6
- lumped_mass: float32 [256, 128], P(('patch', 'sub')), may hold values from 1 to 3
- precond: float32 [256, 128, 128], P(('patch', 'sub'))
Outputs:
- newton_update: float32 [256, 128], P(('patch', 'sub'))
Inputs may be any that keep to these rules, and one draw needn't show every extreme that they name: `owner_block`: at most 16 elements of one device name one block, and some block is named by exactly 16 of one device's elements. `active_counts`: some device has all 512 elements active.
All inputs are finite; a program needn't handle non-finite values.
Results may differ from a plain program's by a relative error of at most 0.0001.
Values sent between devices are 32-bit elements; how exact they have to be, the bound alone decides.
A program may use at most 128 MiB of HBM per device.

v0:
```python
import jax
import jax.numpy as jnp
from jax import lax
from jax.sharding import PartitionSpec as P

SWEEPS = 3


highest = lax.Precision.HIGHEST
conductivity_scale = 0.005


def padded_2(x, sides, width):
    for axis, dim in sides:
        size, length = (lax.axis_size(axis), x.shape[dim])
        up = [(i, (i + 1) % size) for i in range(size - 1)]
        down = [(j, i) for i, j in up]
        last = lax.slice_in_dim(x, length - width, length, axis=dim)
        initial = lax.slice_in_dim(x, 0, width, axis=dim)
        before = lax.ppermute(last, axis, up)
        after = lax.ppermute(initial, axis, down)
        x = jnp.concatenate([before, x, after], axis=dim)
    return x


def element_terms(element_temps, quad_weights, basis_values, basis_grads):
    values = jnp.dot(element_temps, basis_values.T, precision=highest)
    slopes = jnp.einsum("eb,cqb->ecq", element_temps, basis_grads, precision=highest)
    stiff_terms = quad_weights * conductivity_scale * (1.0 + values * values)
    newton_terms = (quad_weights * 2.0 * conductivity_scale * values)[:, None, :] * slopes
    return jnp.concatenate([stiff_terms, newton_terms.reshape(values.shape[0], -1)], axis=1)


def tile_table(basis_values, basis_grads):
    points, functions = basis_values.shape
    stiff_rows = jnp.sum(basis_grads[:, :, :, None] * basis_grads[:, :, None, :], axis=0).reshape(
        points, functions * functions
    )
    newton_rows = (basis_grads[:, :, :, None] * basis_values[None, :, None, :]).reshape(
        3 * points, functions * functions
    )
    return jnp.concatenate([stiff_rows, newton_rows], axis=0)


def interface_pair(iterate, iface_list):
    padded = padded_2(iterate[iface_list], (("patch", 0),), 1)
    return (padded[0], padded[3])


def body(
    element_temps,
    quad_weights,
    basis_values,
    basis_grads,
    owner_block,
    column_ref,
    quadrant,
    active_counts,
    send_list,
    iface_list,
    newton_residual,
    lumped_mass,
    precond,
):
    elements_here = element_temps.shape[0]
    owned = newton_residual.shape[0]
    functions = basis_values.shape[1]
    peers = lax.axis_size("sub")
    capacity = 2 * ((elements_here + owned * peers - 1) // (owned * peers))
    slot_total = peers * owned * capacity
    active = (lax.iota(jnp.int32, elements_here) < active_counts[0]).astype(jnp.float32)
    quad_terms = (
        element_terms(element_temps, quad_weights, basis_values, basis_grads) * active[:, None]
    )
    products = tile_table(basis_values, basis_grads)
    target = owner_block[:, 0]
    hits = (target[:, None] == lax.iota(jnp.int32, peers * owned)[None, :]).astype(jnp.int32)
    position = jnp.sum((jnp.cumsum(hits, axis=0) - hits) * hits, axis=1)
    slot_index = target * capacity + position
    slot_meta = (
        jnp.zeros((slot_total, 2), jnp.int32)
        .at[slot_index]
        .set(jnp.concatenate([column_ref, quadrant], axis=1))
    )
    local_flat = jnp.dot(quad_terms, products, precision=highest)
    tile_slots = (
        jnp.zeros((slot_total, local_flat.shape[1]), jnp.float32).at[slot_index].set(local_flat)
    )
    tile_set, got_meta = (
        lax.all_to_all(tile_slots, "sub", split_axis=0, concat_axis=0, tiled=True),
        lax.all_to_all(slot_meta, "sub", split_axis=0, concat_axis=0, tiled=True),
    )
    tile_set = tile_set.reshape(slot_total, functions, functions)
    row_seg = lax.iota(jnp.int32, slot_total) // capacity % owned * 2 + got_meta[:, 1] // 2
    col_seg = got_meta[:, 0] * 2 + got_meta[:, 1] % 2
    row_picker = (lax.iota(jnp.int32, 2 * owned)[:, None] == row_seg[None, :]).astype(jnp.float32)
    newton_update = jnp.einsum("bij,bj->bi", precond, newton_residual, precision=highest)
    for repeat in range(SWEEPS - 1):
        outgoing = newton_update[send_list]
        ghosts = lax.all_to_all(outgoing, "sub", split_axis=0, concat_axis=0, tiled=True).reshape(
            -1, newton_update.shape[1]
        )
        lower_rows, upper_rows = interface_pair(newton_update, iface_list)
        segments = jnp.concatenate([newton_update, ghosts, lower_rows, upper_rows], axis=0).reshape(
            -1, functions
        )
        row_terms = jnp.einsum("rab,rb->ra", tile_set, segments[col_seg], precision=highest)
        applied = lumped_mass * newton_update + jnp.dot(
            row_picker, row_terms, precision=highest
        ).reshape(owned, -1)
        newton_update = newton_update + jnp.einsum(
            "bij,bj->bi", precond, newton_residual - applied, precision=highest
        )
    return newton_update


def solution(mesh):
    return jax.shard_map(
        body,
        mesh=mesh,
        in_specs=(
            P(("patch", "sub"), None),
            P(("patch", "sub"), None),
            P(),
            P(),
            P(("patch", "sub"), None),
            P(("patch", "sub"), None),
            P(("patch", "sub"), None),
            P(("patch", "sub")),
            P(("patch", "sub"), None),
            P(("patch", "sub"), None),
            P(("patch", "sub"), None),
            P(("patch", "sub"), None),
            P(("patch", "sub"), None, None),
        ),
        out_specs=P(("patch", "sub"), None),
        check_vma=False,
    )
```

profile of v0, /device:TPU:0, one launch (start us, length us, event | category | flops | bytes accessed | tf_op | source)
XLA Modules:
  0.0 623.1 jit_solution(7244988974076981953)
XLA Ops:
  0.0 0.0 copy-start
  0.0 0.0 copy-start.2
  0.0 0.0 copy-start.7
  0.0 0.0 copy-start.8
  0.0 0.8 compare_select_fusion.5
  0.8 0.1 copy.35
  0.9 0.1 reshape.128
  1.0 0.2 copy-done
  1.2 1.6 fusion.33
  2.8 1.2 gather_fusion
  4.0 6.3 %all-to-all-start.2 = ((f32[8,2,128]{2,1,0:T(2,128)}), f32[8,2,128]{2,1,0:T(2,128)S(1)}, u32[]{:S(2)}, u32[]{:S(2)}) async-start(f32[8,2,128]{2,1,0:T(2,128)} %bitcast.16), calls=%async_computation.2 | async-start | bytes 16384 | tf_op jit(solution)/shard_map/all_to_all | solution.py:100
  10.3 0.7 fusion.15
  11.0 1.2 reduce-window.6
  12.2 0.2 slice_reduce_fusion
  12.5 0.8 fusion.13
  13.3 0.7 compare_select_fusion.3
  14.0 5.1 multiply_reduce_fusion
  19.0 0.0 copy-done.4
  19.0 0.3 add_multiply_fusion
  19.3 0.5 convolution_multiply_fusion
  20.4 0.0 copy-done.7
  20.5 0.0 copy-done.8
  20.5 5.9 mul.110
  26.4 1.6 reshape.118
  28.0 0.1 copy.31
  28.2 1.8 scatter_custom_fusion
  30.0 0.8 copy.32
  30.8 0.0 all-to-all-done.2
  30.8 5.3 all-to-all-start
  36.1 10.7 %fusion.2 = f32[512,4096]{1,0:T(8,128)} fusion(f32[192,4096]{1,0:T(8,128)} %mul.110, f32[64,4096]{1,0:T(8,128)} %reshape.118, f32[512,192]{0,1:T(8,128)S(1)} %bitcast.103, f32[512,64]{0,1:T(8,128)S(1)} %get-tuple-element.5, f32[512]{0:T(512)S(1)} %fusion.30), kind=kOutput, calls=%fused_computation.11 | convolution fusion | flops 6443761664 | bytes 13109248 | tf_op jit(solution)/shard_map/dot_general | solution.py:85
  46.8 14.8 %scatter_custom_fusion.1 = f32[1024,4096]{1,0:T(8,128)} fusion(s32[512]{0:T(512)S(1)} %bitcast.118, f32[512,4096]{1,0:T(8,128)} %fusion.2, f32[]{:T(128)} %constant.74.clone.1), kind=kCustom, calls=%fused_computation.8 | custom fusion | bytes 16777728 | tf_op jit(solution)/shard_map/scatter | solution.py:87
  61.5 17.4 %copy.33 = f32[8,128,4096]{1,2,0:T(8,128)} copy(f32[8,128,4096]{2,1,0:T(8,128)} %bitcast.92) | data formatting | bytes 33554432 | tf_op jit(solution)/shard_map/all_to_all | solution.py:90
  79.0 0.0 all-to-all-done
  79.0 5.9 all-to-all-start.1
  84.9 0.1 reshape.136
  85.0 0.6 gather_fusion.1
  85.5 1.3 collective-permute-start.1
  86.8 4.8 collective-permute-start
  91.6 0.0 collective-permute-done.1
  91.6 1.1 collective-permute-done
  92.7 0.1 reshape.121
  92.8 2.8 gather_fusion.2
  95.6 352.9 %all-to-all-done.1 = f32[8,128,4096]{1,2,0:T(8,128)} async-done(((f32[8,128,4096]{1,2,0:T(8,128)}), f32[8,128,4096]{1,2,0:T(8,128)}, u32[]{:S(2)}, u32[]{:S(2)}) %all-to-all-start.1) | async-done | bytes 16777248 | tf_op jit(solution)/shard_map/all_to_all | solution.py:90
  448.5 17.5 %copy.47 = f32[8,128,4096]{2,1,0:T(8,128)} copy(f32[8,128,4096]{1,2,0:T(8,128)} %all-to-all-done.1) | data formatting | bytes 33554432 | tf_op jit(solution)/shard_map/reshape | solution.py:93
  466.0 27.0 %reshape.213 = f32[1024,64,64]{2,1,0:T(8,128)} reshape(f32[8,128,4096]{2,1,0:T(8,128)} %copy.47) | data formatting | bytes 33554432 | tf_op jit(solution)/shard_map/reshape | solution.py:93
  493.0 55.6 %fusion.34 = f32[1024,1,64]{2,1,0:T(1,128)S(1)} fusion(f32[1024,64,64]{2,1,0:T(8,128)} %reshape.213, f32[1024,64,1]{1,2,0:T(1,128)S(1)} %bitcast.100), kind=kOutput, calls=%fused_computation.87 | convolution fusion | flops 50331648 | bytes 17301504 | tf_op jit(solution)/shard_map/rab,rb->ra/dot_general | solution.py:107
  548.7 0.3 fusion.17
  549.0 0.1 reshape.122
  549.1 0.9 fusion.35
  550.0 0.6 gather_fusion.4
  550.6 1.1 gather_fusion.3
  551.7 3.3 all-to-all-start.3
  555.0 1.3 collective-permute-start.3
  556.3 4.8 collective-permute-start.2
  561.1 0.0 collective-permute-done.3
  561.1 1.0 collective-permute-done.2
  562.2 0.0 all-to-all-done.3
  562.2 0.1 reshape.124
  562.2 2.8 gather_fusion.5
  565.1 55.6 %fusion.36 = f32[1024,1,64]{2,1,0:T(1,128)S(1)} fusion(f32[1024,64,64]{2,1,0:T(8,128)} %reshape.213, f32[1024,64,1]{1,2,0:T(1,128)S(1)} %bitcast.101), kind=kOutput, calls=%fused_computation.89 | convolution fusion | flops 50331648 | bytes 17301504 | tf_op jit(solution)/shard_map/rab,rb->ra/dot_general | solution.py:107
  620.7 0.3 fusion.16
  621.0 0.1 reshape.125
  621.1 0.9 fusion.37
  622.0 0.6 add.90
  (29 shorter events, 0.2 us)
Async XLA Ops:
  0.0 1.2 copy-start
  0.0 19.3 %copy-start.1 = (f32[3,64,64]{2,1,0:T(8,128)S(1)}, f32[3,64,64]{2,1,0:T(8,128)}, u32[]{:S(2)}) copy-start(f32[3,64,64]{2,1,0:T(8,128)} %param.16) | copy-start | bytes 147460
  0.0 19.0 %copy-start.3 = (f32[64,64]{1,0:T(8,128)S(1)}, f32[64,64]{1,0:T(8,128)}, u32[]{:S(2)}) copy-start(f32[64,64]{1,0:T(8,128)} %param.15) | copy-start | bytes 49156
  0.0 19.0 %copy-start.4 = (f32[512,64]{0,1:T(8,128)S(1)}, f32[512,64]{0,1:T(8,128)}, u32[]{:S(2)}) copy-start(f32[512,64]{0,1:T(8,128)} %param.14) | copy-start | bytes 393220
  0.0 19.0 %copy-start.2 = (f32[512,64]{0,1:T(8,128)S(1)}, f32[512,64]{0,1:T(8,128)}, u32[]{:S(2)}) copy-start(f32[512,64]{0,1:T(8,128)} %param.13) | copy-start | bytes 393220
  0.0 20.4 %copy-start.7 = (s32[512,1]{0,1:T(1,128)S(1)}, s32[512,1]{0,1:T(1,128)}, u32[]{:S(2)}) copy-start(s32[512,1]{0,1:T(1,128)} %param.19) | copy-start | bytes 6148
  0.0 20.4 %copy-start.8 = (s32[512,1]{0,1:T(1,128)S(1)}, s32[512,1]{0,1:T(1,128)}, u32[]{:S(2)}) copy-start(s32[512,1]{0,1:T(1,128)} %param.18) | copy-start | bytes 6148
  4.0 26.8 %all-to-all-start.2 = ((f32[8,2,128]{2,1,0:T(2,128)}), f32[8,2,128]{2,1,0:T(2,128)S(1)}, u32[]{:S(2)}, u32[]{:S(2)}) async-start(f32[8,2,128]{2,1,0:T(2,128)} %bitcast.16), calls=%async_computation.2 | async-start | bytes 16384 | tf_op jit(solution)/shard_map/all_to_all | solution.py:100
  30.8 48.2 %all-to-all-start = ((s32[8,128,2]{1,2,0:T(2,128)}), s32[8,128,2]{1,2,0:T(2,128)S(1)}, u32[]{:S(2)}, u32[]{:S(2)}) async-start(s32[8,128,2]{1,2,0:T(2,128)} %copy.32), calls=%async_computation | async-start | bytes 16384 | tf_op jit(solution)/shard_map/all_to_all | solution.py:91
  79.0 5.9 copy-start.9
  79.0 369.5 %all-to-all-start.1 = ((f32[8,128,4096]{1,2,0:T(8,128)}), f32[8,128,4096]{1,2,0:T(8,128)}, u32[]{:S(2)}, u32[]{:S(2)}) async-start(f32[8,128,4096]{1,2,0:T(8,128)} %copy.33), calls=%async_computation.1 | async-start | bytes 33554432 | tf_op jit(solution)/shard_map/all_to_all | solution.py:90
  85.5 6.1 collective-permute-start.1
  86.8 5.8 collective-permute-start
  493.0 56.0 %copy-start.5 = (f32[8,128]{1,0:T(8,128)S(1)}, f32[8,128]{1,0:T(8,128)}, u32[]{:S(2)}) copy-start(f32[8,128]{1,0:T(8,128)} %param.23) | copy-start | bytes 12292
  493.0 56.0 %copy-start.6 = (f32[8,128]{1,0:T(8,128)S(1)}, f32[8,128]{1,0:T(8,128)}, u32[]{:S(2)}) copy-start(f32[8,128]{1,0:T(8,128)} %param.24) | copy-start | bytes 12292
  551.7 10.5 %all-to-all-start.3 = ((f32[8,2,128]{2,1,0:T(2,128)}), f32[8,2,128]{2,1,0:T(2,128)S(1)}, u32[]{:S(2)}, u32[]{:S(2)}) async-start(f32[8,2,128]{2,1,0:T(2,128)} %bitcast.31), calls=%async_computation.3 | async-start | bytes 16384 | tf_op jit(solution)/shard_map/all_to_all | solution.py:100
  555.0 6.1 collective-permute-start.3
  556.3 5.9 collective-permute-start.2
where the time goes:
time: 631 us; the launch traced here: 623 us
  waiting for transfers between devices  355 us (56%)
  matrix products  127 us (20%)
  local copies, waits for them, and re-layouts  97.1 us (15%)
  starting transfers between devices  32.9 us (5%)
  other arithmetic  9.97 us (2%)
    all_to_all x1, waiting for transfers between devices, body(): lax.all_to_all(tile_slots, 'sub', split_axis=0, concat_axis=0, tiled=True)  353 us
    dot_general x2, matrix products, body(): jnp.einsum('rab,rb->ra', tile_set, segments[col_seg], precision=highest)  111 us
    reshape x2, local copies, waits for them, and re-layouts, body(): tile_set = tile_set.reshape(slot_total, functions, functions)  44.5 us
    all_to_all x1, local copies, waits for them, and re-layouts, body(): lax.all_to_all(tile_slots, 'sub', split_axis=0, concat_axis=0, tiled=True)  17.4 us
    scatter x1, local copies, waits for them, and re-layouts, body(): jnp.zeros((slot_total, local_flat.shape[1]), jnp.float32).at[slot_index]  14.8 us
  transfers between devices with their start and end apart: 8, of which 3 were waited for; matrix products, arithmetic and copies ran while one was open for 11% of the time, Pallas kernels for 0%

commit v1 on v0

v1 whole, which is shorter than its diff:
```python
import functools

import jax
import jax.numpy as jnp
from jax import lax
from jax.experimental import pallas as pl
from jax.experimental.pallas import tpu as pltpu
from jax.sharding import PartitionSpec as P

SWEEPS = 3
CONDUCTIVITY = 0.005
MESH = pl.DeviceIdType.MESH
F32 = jnp.float32
BF16 = jnp.bfloat16


def halves(x):
    head = x.astype(BF16).astype(F32)
    return head, x - head


def log2(n):
    assert n & (n - 1) == 0
    return n.bit_length() - 1


def dot(a, b):
    return jnp.dot(a, b, preferred_element_type=F32)


def dot_nt(a, b):
    return lax.dot_general(a, b, (((1,), (1,)), ((), ())), preferred_element_type=F32)


def kernel(
    dims,
    temps,
    weights,
    values,
    grads,
    owner,
    column,
    quadrant,
    counts,
    sends,
    ifaces,
    residual,
    mass,
    precond,
    out,
    ext,
    ifb,
    ub,
    rows_out,
    rows_in,
    pick,
    put,
    terms,
    ph,
    plo,
    ag_send,
    ag_recv,
    if_send,
    if_recv,
    rs_send,
    rs_recv,
):
    n_patch, n_sub, nbd, gh, ig, erows, base, nbp, rbp = dims
    patch, sub = lax.axis_index("patch"), lax.axis_index("sub")
    upper = lax.rem(patch + 1, n_patch)
    lower = lax.rem(patch + n_patch - 1, n_patch)
    peers = [lax.rem(sub + k, n_sub) for k in range(1, n_sub)]
    sources = [lax.rem(sub + n_sub - k, n_sub) for k in range(1, n_sub)]
    everyone = [lax.rem(sub + k, n_sub) for k in range(n_sub)]

    barrier = pltpu.get_barrier_semaphore()
    for peer in peers:
        pl.semaphore_signal(barrier, inc=1, device_id=(patch, peer), device_id_type=MESH)
    for other in (upper, lower):
        for peer in everyone:
            pl.semaphore_signal(barrier, inc=1, device_id=(other, peer), device_id_type=MESH)

    def solve(r):
        head, rest = halves(r)
        both = jnp.concatenate([head, rest], axis=0).astype(BF16)
        wide = dot_nt(both, ph[...]) + dot_nt(both, plo[...])
        wide = wide[:nbd] + wide[nbd:]
        row = lax.broadcasted_iota(jnp.int32, (nbd, 128), 0)
        total = jnp.zeros((nbd, 128), F32)
        for b in range(nbd):
            total = total + jnp.where(row == b, wide[:, b * 128 : (b + 1) * 128], 0.0)
        return total

    def expand(u, sweep):
        ub[sweep] = u
        first = pl.multiple_of(sub * erows, 8)
        ext[sweep, pl.ds(first, nbd), :] = u
        for o in range(n_sub):
            for j in range(gh):
                ext[sweep, pl.ds(first + (nbd + o * gh + j), 1), :] = ub[
                    sweep, pl.ds(sends[j, o], 1), :
                ]
        for side in range(2):
            for j in range(ig):
                ifb[sweep, pl.ds(side * ig + j, 1), :] = ub[sweep, pl.ds(ifaces[side, j], 1), :]

    def spread(sweep):
        copies = []
        mine = pl.ds(pl.multiple_of(sub * erows, 8), erows)
        for side, other in ((0, upper), (1, lower)):
            place = pl.ds(pl.multiple_of(base + (side * n_sub + sub) * 2 * ig, 8), 2 * ig)
            for k, peer in enumerate(everyone):
                copies.append(
                    pltpu.make_async_remote_copy(
                        src_ref=ifb.at[sweep],
                        dst_ref=ext.at[sweep, place],
                        send_sem=if_send.at[sweep, side, k],
                        recv_sem=if_recv.at[sweep, side, sub],
                        device_id=(other, peer),
                        device_id_type=MESH,
                    )
                )
        for k, peer in enumerate(peers):
            copies.append(
                pltpu.make_async_remote_copy(
                    src_ref=ext.at[sweep, mine],
                    dst_ref=ext.at[sweep, mine],
                    send_sem=ag_send.at[sweep, k],
                    recv_sem=ag_recv.at[sweep, sub],
                    device_id=(patch, peer),
                    device_id_type=MESH,
                )
            )
        for copy in copies:
            copy.start()
        return copies

    def gathered(sweep):
        for k, source in enumerate(sources):
            place = pl.ds(pl.multiple_of(source * erows, 8), erows)
            pltpu.make_async_remote_copy(
                src_ref=ext.at[sweep, place],
                dst_ref=ext.at[sweep, place],
                send_sem=ag_send.at[sweep, k],
                recv_sem=ag_recv.at[sweep, source],
                device_id=(patch, source),
                device_id_type=MESH,
            ).wait_recv()
        for side in range(2):
            for s in range(n_sub):
                pltpu.make_async_remote_copy(
                    src_ref=ifb.at[sweep],
                    dst_ref=ext.at[sweep, pl.ds(base + (side * n_sub + s) * 2 * ig, 2 * ig)],
                    send_sem=if_send.at[sweep, side, s],
                    recv_sem=if_recv.at[sweep, side, s],
                    device_id=(lower, s),
                    device_id_type=MESH,
                ).wait_recv()

    r = residual[...]
    p_all = precond[...].reshape(nbd * 128, 128)
    p_head = p_all.astype(BF16)
    ph[...] = p_head
    plo[...] = (p_all - p_head.astype(F32)).astype(BF16)
    used = base + 4 * ig * n_sub
    if nbp > used:
        for sweep in range(SWEEPS - 1):
            ext[sweep, pl.ds(used, nbp - used), :] = jnp.zeros((nbp - used, 128), F32)
    u = solve(r)
    expand(u, 0)
    pl.semaphore_wait(barrier, n_sub - 1 + 2 * n_sub)
    copies = spread(0)

    points, functions = values.shape
    elements = temps.shape[1]
    g3 = grads[...].reshape(3 * points, functions)
    g_head, g_rest = halves(jnp.concatenate([g3, values[...]], axis=0))
    left = jnp.concatenate([g_head, g_head, g_rest, g_rest], axis=1).astype(BF16)
    h3, l3 = g_head[: 3 * points], g_rest[: 3 * points]
    back = jnp.transpose(jnp.concatenate([h3, h3, l3, l3], axis=0)).astype(BF16)
    t_head, t_rest = halves(temps[...])
    four = jnp.concatenate([t_head, t_rest, t_head, t_rest], axis=0).astype(BF16)
    fields = dot(left, four)
    vals = fields[3 * points :]
    w = weights[...]
    terms[pl.ds(0, points), :] = w * CONDUCTIVITY * (1.0 + vals * vals)
    slope_weight = w * (2.0 * CONDUCTIVITY) * vals
    for c in range(3):
        terms[pl.ds((c + 1) * points, points), :] = (
            slope_weight * fields[c * points : (c + 1) * points]
        )
    block, col, quad = owner[...], column[...], quadrant[...]
    o = block >> log2(nbd)
    near = col - nbd
    far = near - n_sub * gh
    side = far >> log2(ig)
    own_place = o * erows + col
    near_place = (near >> log2(gh)) * erows + nbd + o * gh + (near & (gh - 1))
    far_place = base + (side * n_sub + o) * 2 * ig + (1 - side) * ig + (far & (ig - 1))
    neighbour = patch - 1 + 2 * side
    far_place = jnp.where((neighbour >= 0) & (neighbour < n_patch), far_place, -2 * nbp)
    place = jnp.where(near < 0, own_place, jnp.where(far < 0, near_place, far_place))
    place = place + (quad & 1) * nbp
    active = lax.broadcasted_iota(jnp.int32, (1, elements), 1) < counts[0]
    target = jnp.where(active, block + (quad >> 1) * rbp, -1)
    for i in range(2 * nbp // 128):
        index = lax.broadcasted_iota(jnp.int32, (128, elements), 0) + i * 128
        pick[pl.ds(i * 128, 128), :] = jnp.where(index == place, 1.0, 0.0).astype(BF16)
    for i in range(2 * rbp // 128):
        index = lax.broadcasted_iota(jnp.int32, (128, elements), 0) + i * 128
        put[pl.ds(i * 128, 128), :] = jnp.where(index == target, 1.0, 0.0).astype(BF16)

    for sweep in range(SWEEPS - 1):
        gathered(sweep)
        flat = jnp.transpose(ext[sweep])
        head, rest = halves(flat)
        segments = jnp.concatenate(
            [
                jnp.concatenate([head[:functions], head[functions:]], axis=1),
                jnp.concatenate([rest[:functions], rest[functions:]], axis=1),
            ],
            axis=0,
        ).astype(BF16)
        x = dot(segments, pick[...]).astype(BF16)
        gx = dot(left, jnp.concatenate([x, x], axis=0))
        vx = gx[3 * points :]
        k0 = terms[pl.ds(0, points), :]
        flux = jnp.concatenate(
            [
                k0 * gx[c * points : (c + 1) * points]
                + terms[pl.ds((c + 1) * points, points), :] * vx
                for c in range(3)
            ],
            axis=0,
        )
        f_head, f_rest = halves(flux)
        z = dot_nt(jnp.concatenate([f_head, f_rest], axis=0).astype(BF16), put[...])
        z_head, z_rest = halves(z[: 3 * points] + z[3 * points :])
        rt = dot(back, jnp.concatenate([z_head, z_rest, z_head, z_rest], axis=0).astype(BF16))
        rows_out[sweep] = jnp.transpose(jnp.concatenate([rt[:, :rbp], rt[:, rbp:]], axis=0))
        for k, peer in enumerate(peers):
            copy = pltpu.make_async_remote_copy(
                src_ref=rows_out.at[sweep, pl.ds(pl.multiple_of(peer * nbd, 8), nbd)],
                dst_ref=rows_in.at[sweep, sub],
                send_sem=rs_send.at[sweep, k],
                recv_sem=rs_recv.at[sweep, sub],
                device_id=(patch, peer),
                device_id_type=MESH,
            )
            copy.start()
            copies.append(copy)
        applied = mass[...] * u + rows_out[sweep, pl.ds(pl.multiple_of(sub * nbd, 8), nbd), :]
        for k, source in enumerate(sources):
            pltpu.make_async_remote_copy(
                src_ref=rows_in.at[sweep, source],
                dst_ref=rows_in.at[sweep, source],
                send_sem=rs_send.at[sweep, k],
                recv_sem=rs_recv.at[sweep, source],
                device_id=(patch, source),
                device_id_type=MESH,
            ).wait_recv()
            applied = applied + rows_in[sweep, source]
        u = u + solve(r - applied)
        if sweep < SWEEPS - 2:
            expand(u, sweep + 1)
            copies += spread(sweep + 1)
    out[...] = u
    for copy in copies:
        copy.wait_send()


def body(
    element_temps,
    quad_weights,
    basis_values,
    basis_grads,
    owner_block,
    column_ref,
    quadrant,
    active_counts,
    send_list,
    iface_list,
    newton_residual,
    lumped_mass,
    precond,
):
    n_patch, n_sub = lax.axis_size("patch"), lax.axis_size("sub")
    nbd, points = newton_residual.shape
    gh, ig = send_list.shape[1], iface_list.shape[1]
    elements = element_temps.shape[0]
    quads = basis_values.shape[0]
    erows = -(-(nbd + n_sub * gh) // 8) * 8
    base = n_sub * erows
    nbp = -(-(base + 4 * ig * n_sub) // 128) * 128
    rbp = -(-(n_sub * nbd) // 128) * 128
    dims = (n_patch, n_sub, nbd, gh, ig, erows, base, nbp, rbp)
    steps = SWEEPS - 1
    vmem = pl.BlockSpec(memory_space=pltpu.VMEM)
    smem = pl.BlockSpec(memory_space=pltpu.SMEM)
    dma = pltpu.SemaphoreType.DMA
    return pl.pallas_call(
        functools.partial(kernel, dims),
        out_shape=jax.ShapeDtypeStruct((nbd, points), F32),
        in_specs=[vmem] * 7 + [smem] * 3 + [vmem] * 3,
        out_specs=vmem,
        scratch_shapes=[
            pltpu.VMEM((steps, nbp, points), F32),
            pltpu.VMEM((steps, 2 * ig, points), F32),
            pltpu.VMEM((steps, nbd, points), F32),
            pltpu.VMEM((steps, rbp, points), F32),
            pltpu.VMEM((steps, n_sub, nbd, points), F32),
            pltpu.VMEM((2 * nbp, elements), BF16),
            pltpu.VMEM((2 * rbp, elements), BF16),
            pltpu.VMEM((4 * quads, elements), F32),
            pltpu.VMEM((nbd * points, points), BF16),
            pltpu.VMEM((nbd * points, points), BF16),
            dma((steps, n_sub)),
            dma((steps, n_sub)),
            dma((steps, 2, n_sub)),
            dma((steps, 2, n_sub)),
            dma((steps, n_sub)),
            dma((steps, n_sub)),
        ],
        compiler_params=pltpu.CompilerParams(
            collective_id=0, has_side_effects=True, vmem_limit_bytes=32 * 1024 * 1024
        ),
    )(
        element_temps.T,
        quad_weights.T,
        basis_values,
        basis_grads,
        owner_block.reshape(1, elements),
        column_ref.reshape(1, elements),
        quadrant.reshape(1, elements),
        active_counts,
        send_list.T,
        iface_list,
        newton_residual,
        lumped_mass,
        precond,
    )


def solution(mesh):
    return jax.shard_map(
        body,
        mesh=mesh,
        in_specs=(
            P(("patch", "sub"), None),
            P(("patch", "sub"), None),
            P(),
            P(),
            P(("patch", "sub"), None),
            P(("patch", "sub"), None),
            P(("patch", "sub"), None),
            P(("patch", "sub")),
            P(("patch", "sub"), None),
            P(("patch", "sub"), None),
            P(("patch", "sub"), None),
            P(("patch", "sub"), None),
            P(("patch", "sub"), None, None),
        ),
        out_specs=P(("patch", "sub"), None),
        check_vma=False,
    )
```

time: 631 us -> 37.9 us (0.06); the launches traced: 623 us -> 37.5 us
  waiting for transfers between devices: 355 us -> 0 us
  matrix products: 127 us -> 0 us
  local copies, waits for them, and re-layouts: 97.1 us -> 7.14 us
  starting transfers between devices: 32.9 us -> 0 us
  Pallas kernels: 0 us -> 29.7 us
  other arithmetic: 9.97 us -> 0 us
    all_to_all x4 -> x0, waiting for transfers between devices: 353 us -> none  [the longest x1 353 us: body(): lax.all_to_all(tile_slots, 'sub', split_axis=0, concat_axis=0, tiled=True)]
    dot_general x10 -> x0, matrix products: 127 us -> none  [the longest x2 111 us: body(): jnp.einsum('rab,rb->ra', tile_set, segments[col_seg], precision=highest)]
    reshape x7 -> x0, local copies, waits for them, and re-layouts: 46.5 us -> none  [the longest x2 44.5 us: body(): tile_set = tile_set.reshape(slot_total, functions, functions)]
    pallas_call x0 -> x1, Pallas kernels: none -> 29.7 us  [body(): pl.pallas_call(functools.partial(kernel, dims), out_shape=jax.ShapeDtypeS...]
    all_to_all x4 -> x0, starting transfers between devices: 20.8 us -> none  [the longest x2 9.58 us: body(): lax.all_to_all(outgoing, 'sub', split_axis=0, concat_axis=0, tiled=True)]
    all_to_all x2 -> x0, local copies, waits for them, and re-layouts: 18.2 us -> none  [the longest x1 17.4 us: body(): lax.all_to_all(tile_slots, 'sub', split_axis=0, concat_axis=0, tiled=True)]
    scatter x2 -> x0, local copies, waits for them, and re-layouts: 16.6 us -> none  [the longest x1 14.8 us: body(): jnp.zeros((slot_total, local_flat.shape[1]), jnp.float32).at[slot_index]]
    ppermute x4 -> x0, starting transfers between devices: 12.2 us -> none  [the longest x2 9.58 us: padded_2(): before = lax.ppermute(last, axis, up)]
  transfers between devices with their start and end apart: 8 -> 0, of which waited for: 3 -> 0; matrix products, arithmetic and copies ran while one was open for 11% -> 0% of each run, Pallas kernels for 0% -> 0%
where the time goes in v1:
time: 37.9 us; the launch traced here: 37.5 us
  Pallas kernels  29.7 us (78%)
  local copies, waits for them, and re-layouts  7.14 us (19%)
  between operations  0.72 us (2%)
    pallas_call x1, Pallas kernels, body(): pl.pallas_call(functools.partial(kernel, dims), out_shape=jax.ShapeDtypeS...  29.7 us
    unnamed x25, local copies, waits for them, and re-layouts  7.14 us

profile of v1, /device:TPU:0, one launch (start us, length us, event | category | flops | bytes accessed | tf_op | source)
XLA Modules:
  0.0 37.5 jit_solution(9386106068799595956)
XLA Ops:
  0.0 0.0 copy-start.8
  0.7 0.0 copy-start.7
  0.7 0.0 copy-start.6
  0.7 0.0 copy-start.5
  0.7 0.0 copy-start.10
  0.7 0.0 copy-done.8
  0.7 0.6 %copy-done.7 = s32[512,1]{0,1:T(1,128)S(1)} copy-done((s32[512,1]{0,1:T(1,128)S(1)}, s32[512,1]{0,1:T(1,128)}, u32[]{:S(2)}) %copy-start.7) | copy-done | bytes 2072
  1.4 0.0 copy-done.6
  1.4 0.0 copy-done.5
  1.4 0.0 copy-done.10
  1.4 0.0 copy-start
  1.4 1.0 %copy-done = f32[8,128,128]{2,1,0:T(8,128)S(1)} copy-done((f32[8,128,128]{2,1,0:T(8,128)S(1)}, f32[8,128,128]{2,1,0:T(8,128)}, u32[]{:S(2)}) %copy-start) | copy-done | bytes 524312
  2.4 0.0 copy-start.1
  2.4 0.9 %copy-done.1 = f32[512,64]{0,1:T(8,128)S(1)} copy-done((f32[512,64]{0,1:T(8,128)S(1)}, f32[512,64]{0,1:T(8,128)}, u32[]{:S(2)}) %copy-start.1) | copy-done | bytes 131096
  3.3 0.0 copy-start.2
  3.3 0.9 %copy-done.2 = f32[512,64]{0,1:T(8,128)S(1)} copy-done((f32[512,64]{0,1:T(8,128)S(1)}, f32[512,64]{0,1:T(8,128)}, u32[]{:S(2)}) %copy-start.2) | copy-done | bytes 131096
  4.2 0.0 copy-start.3
  4.2 0.9 %copy-done.3 = f32[3,64,64]{2,1,0:T(8,128)S(1)} copy-done((f32[3,64,64]{2,1,0:T(8,128)S(1)}, f32[3,64,64]{2,1,0:T(8,128)}, u32[]{:S(2)}) %copy-start.3) | copy-done | bytes 49176
  5.1 0.0 copy-start.4
  5.1 0.8 %copy-done.4 = f32[64,64]{1,0:T(8,128)S(1)} copy-done((f32[64,64]{1,0:T(8,128)S(1)}, f32[64,64]{1,0:T(8,128)}, u32[]{:S(2)}) %copy-start.4) | copy-done | bytes 16408
  5.9 0.0 copy-start.9
  5.9 0.7 %copy-done.9 = s32[512,1]{0,1:T(1,128)S(1)} copy-done((s32[512,1]{0,1:T(1,128)S(1)}, s32[512,1]{0,1:T(1,128)}, u32[]{:S(2)}) %copy-start.9) | copy-done | bytes 2072
  6.6 0.0 copy-start.11
  6.6 0.7 %copy-done.11 = s32[2,4]{1,0:T(2,128)S(1)} copy-done((s32[2,4]{1,0:T(2,128)S(1)}, s32[2,4]{1,0:T(2,128)}, u32[]{:S(2)}) %copy-start.11) | copy-done | bytes 56
  7.3 29.7 %shard_map.127 = f32[8,128]{1,0:T(8,128)S(1)} custom-call(f32[64,512]{1,0:T(8,128)S(1)} %bitcast.6, f32[64,512]{1,0:T(8,128)S(1)} %bitcast.7, f32[64,64]{1,0:T(8,128)S(1)} %copy-done.4, f32[3,64,64]{2,1,0:T(8,128)S(1)} %copy-done.3, s32[1,512]{1,0:T(1,128)S(1)} %bitcast.8, s32[1,512]{1,0:T(1,128)S(1)} %bitcast.9, s32[1,512]{1,0:T(1,128)S(1)} %bitcast.10, ...), custom_call_target="tpu_custom_call" | custom-call | tf_op jit(solution)/shard_map/pallas_call | solution.py:301
  36.9 0.6 %copy.16 = f32[8,128]{1,0:T(8,128)} copy(f32[8,128]{1,0:T(8,128)S(1)} %shard_map.127) | data formatting | bytes 8192
Async XLA Ops:
  0.0 0.7 %copy-start.8 = (s32[512,1]{0,1:T(1,128)S(1)}, s32[512,1]{0,1:T(1,128)}, u32[]{:S(2)}) copy-start(s32[512,1]{0,1:T(1,128)} %param.18) | copy-start | bytes 6148
  0.7 0.7 %copy-start.7 = (s32[512,1]{0,1:T(1,128)S(1)}, s32[512,1]{0,1:T(1,128)}, u32[]{:S(2)}) copy-start(s32[512,1]{0,1:T(1,128)} %param.17) | copy-start | bytes 6148
  0.7 0.7 %copy-start.6 = (f32[8,128]{1,0:T(8,128)S(1)}, f32[8,128]{1,0:T(8,128)}, u32[]{:S(2)}) copy-start(f32[8,128]{1,0:T(8,128)} %mass.1) | copy-start | bytes 12292
  0.7 0.7 %copy-start.5 = (f32[8,128]{1,0:T(8,128)S(1)}, f32[8,128]{1,0:T(8,128)}, u32[]{:S(2)}) copy-start(f32[8,128]{1,0:T(8,128)} %residual.1) | copy-start | bytes 12292
  0.7 0.7 %copy-start.10 = (s32[8,2]{0,1:T(2,128)S(1)}, s32[8,2]{0,1:T(2,128)}, u32[]{:S(2)}) copy-start(s32[8,2]{0,1:T(2,128)} %param.21) | copy-start | bytes 196
  1.4 1.0 %copy-start = (f32[8,128,128]{2,1,0:T(8,128)S(1)}, f32[8,128,128]{2,1,0:T(8,128)}, u32[]{:S(2)}) copy-start(f32[8,128,128]{2,1,0:T(8,128)} %precond.1) | copy-start | bytes 1572868
  2.4 0.9 %copy-start.1 = (f32[512,64]{0,1:T(8,128)S(1)}, f32[512,64]{0,1:T(8,128)}, u32[]{:S(2)}) copy-start(f32[512,64]{0,1:T(8,128)} %param.13) | copy-start | bytes 393220
  3.3 0.9 %copy-start.2 = (f32[512,64]{0,1:T(8,128)S(1)}, f32[512,64]{0,1:T(8,128)}, u32[]{:S(2)}) copy-start(f32[512,64]{0,1:T(8,128)} %param.14) | copy-start | bytes 393220
  4.2 0.9 %copy-start.3 = (f32[3,64,64]{2,1,0:T(8,128)S(1)}, f32[3,64,64]{2,1,0:T(8,128)}, u32[]{:S(2)}) copy-start(f32[3,64,64]{2,1,0:T(8,128)} %grads.1) | copy-start | bytes 147460
  5.1 0.8 %copy-start.4 = (f32[64,64]{1,0:T(8,128)S(1)}, f32[64,64]{1,0:T(8,128)}, u32[]{:S(2)}) copy-start(f32[64,64]{1,0:T(8,128)} %values.1) | copy-start | bytes 49156
  5.9 0.7 %copy-start.9 = (s32[512,1]{0,1:T(1,128)S(1)}, s32[512,1]{0,1:T(1,128)}, u32[]{:S(2)}) copy-start(s32[512,1]{0,1:T(1,128)} %param.19) | copy-start | bytes 6148
  6.6 0.7 %copy-start.11 = (s32[2,4]{1,0:T(2,128)S(1)}, s32[2,4]{1,0:T(2,128)}, u32[]{:S(2)}) copy-start(s32[2,4]{1,0:T(2,128)} %ifaces.1) | copy-start | bytes 100

commit v2 on v1

--- a/solution.py
+++ b/solution.py
@@ -34,6 +34,20 @@
 
 def kernel(
     dims,
+    temps_in,
+    weights_in,
+    values_in,
+    grads_in,
+    owner_in,
+    column_in,
+    quadrant_in,
+    counts_in,
+    sends_in,
+    ifaces_in,
+    residual_in,
+    mass_in,
+    precond_in,
+    out,
     temps,
     weights,
     values,
@@ -47,7 +61,7 @@
     residual,
     mass,
     precond,
-    out,
+    load_sem,
     ext,
     ifb,
     ub,
@@ -73,6 +87,26 @@
     sources = [lax.rem(sub + n_sub - k, n_sub) for k in range(1, n_sub)]
     everyone = [lax.rem(sub + k, n_sub) for k in range(n_sub)]
 
+    pairs = (
+        (residual_in, residual),
+        (sends_in, sends),
+        (ifaces_in, ifaces),
+        (precond_in, precond),
+        (temps_in, temps),
+        (grads_in, grads),
+        (values_in, values),
+        (weights_in, weights),
+        (owner_in, owner),
+        (column_in, column),
+        (quadrant_in, quadrant),
+        (counts_in, counts),
+        (mass_in, mass),
+    )
+    loads = [
+        pltpu.make_async_copy(given, held, load_sem.at[i]) for i, (given, held) in enumerate(pairs)
+    ]
+    for load in loads:
+        load.start()
     barrier = pltpu.get_barrier_semaphore()
     for peer in peers:
         pl.semaphore_signal(barrier, inc=1, device_id=(patch, peer), device_id_type=MESH)
@@ -157,6 +191,8 @@
                     device_id_type=MESH,
                 ).wait_recv()
 
+    for load in loads[:4]:
+        load.wait()
     r = residual[...]
     p_all = precond[...].reshape(nbd * 128, 128)
     p_head = p_all.astype(BF16)
@@ -171,6 +207,8 @@
     pl.semaphore_wait(barrier, n_sub - 1 + 2 * n_sub)
     copies = spread(0)
 
+    for load in loads[4:]:
+        load.wait()
     points, functions = values.shape
     elements = temps.shape[1]
     g3 = grads[...].reshape(3 * points, functions)
@@ -201,7 +239,7 @@
     far_place = jnp.where((neighbour >= 0) & (neighbour < n_patch), far_place, -2 * nbp)
     place = jnp.where(near < 0, own_place, jnp.where(far < 0, near_place, far_place))
     place = place + (quad & 1) * nbp
-    active = lax.broadcasted_iota(jnp.int32, (1, elements), 1) < counts[0]
+    active = lax.broadcasted_iota(jnp.int32, (1, elements), 1) < counts[...]
     target = jnp.where(active, block + (quad >> 1) * rbp, -1)
     for i in range(2 * nbp // 128):
         index = lax.broadcasted_iota(jnp.int32, (128, elements), 0) + i * 128
@@ -296,14 +334,28 @@
     dims = (n_patch, n_sub, nbd, gh, ig, erows, base, nbp, rbp)
     steps = SWEEPS - 1
     vmem = pl.BlockSpec(memory_space=pltpu.VMEM)
-    smem = pl.BlockSpec(memory_space=pltpu.SMEM)
+    hbm = pl.BlockSpec(memory_space=pltpu.HBM)
     dma = pltpu.SemaphoreType.DMA
     return pl.pallas_call(
         functools.partial(kernel, dims),
         out_shape=jax.ShapeDtypeStruct((nbd, points), F32),
-        in_specs=[vmem] * 7 + [smem] * 3 + [vmem] * 3,
+        in_specs=[hbm] * 13,
         out_specs=vmem,
         scratch_shapes=[
+            pltpu.VMEM(element_temps.shape[::-1], F32),
+            pltpu.VMEM(quad_weights.shape[::-1], F32),
+            pltpu.VMEM(basis_values.shape, F32),
+            pltpu.VMEM(basis_grads.shape, F32),
+            pltpu.VMEM((1, elements), jnp.int32),
+            pltpu.VMEM((1, elements), jnp.int32),
+            pltpu.VMEM((1, elements), jnp.int32),
+            pltpu.VMEM((1, 1), jnp.int32),
+            pltpu.SMEM(send_list.shape[::-1], jnp.int32),
+            pltpu.SMEM(iface_list.shape, jnp.int32),
+            pltpu.VMEM(newton_residual.shape, F32),
+            pltpu.VMEM(lumped_mass.shape, F32),
+            pltpu.VMEM(precond.shape, F32),
+            dma((13,)),
             pltpu.VMEM((steps, nbp, points), F32),
             pltpu.VMEM((steps, 2 * ig, points), F32),
             pltpu.VMEM((steps, nbd, points), F32),
@@ -322,7 +374,7 @@
             dma((steps, n_sub)),
         ],
         compiler_params=pltpu.CompilerParams(
-            collective_id=0, has_side_effects=True, vmem_limit_bytes=32 * 1024 * 1024
+            collective_id=0, has_side_effects=True, vmem_limit_bytes=56 * 1024 * 1024
         ),
     )(
         element_temps.T,
@@ -332,7 +384,7 @@
         owner_block.reshape(1, elements),
         column_ref.reshape(1, elements),
         quadrant.reshape(1, elements),
-        active_counts,
+        active_counts.reshape(1, 1),
         send_list.T,
         iface_list,
         newton_residual,

time: 37.9 us -> 32 us (0.84)
  local copies, waits for them, and re-layouts: 7.14 us -> 1.28 us
    unnamed x25 -> x1, local copies, waits for them, and re-layouts: 7.14 us -> 1.28 us
where the time goes in v2:
time: 32 us; the launch traced here: 31.8 us
  Pallas kernels  29.9 us (93%)
  local copies, waits for them, and re-layouts  1.28 us (4%)
  between operations  0.66 us (2%)
    pallas_call x1, Pallas kernels, body(): pl.pallas_call(functools.partial(kernel, dims), out_shape=jax.ShapeDtypeS...  29.9 us
    unnamed x1, local copies, waits for them, and re-layouts  1.28 us

profile of v2, /device:TPU:0, one launch (start us, length us, event | category | flops | bytes accessed | tf_op | source)
XLA Modules:
  0.0 31.8 jit_solution(9308878940115137353)
XLA Ops:
  0.7 29.9 %shard_map.127 = f32[8,128]{1,0:T(8,128)} custom-call(f32[64,512]{1,0:T(8,128)} %bitcast.8, f32[64,512]{1,0:T(8,128)} %bitcast.9, f32[64,64]{1,0:T(8,128)} %values_in.1, f32[3,64,64]{2,1,0:T(8,128)} %grads_in.1, s32[1,512]{1,0:T(1,128)} %bitcast.10, s32[1,512]{1,0:T(1,128)} %bitcast.11, s32[1,512]{1,0:T(1,128)} %bitcast.12, s32[1,1]{1,0:T(1,128)} %bitcast.7.counts_in, ...), custom_call_target="tpu_custom_call" | custom-call | tf_op jit(solution)/shard_map/pallas_call | solution.py:339
  30.5 1.3 %copy.16 = f32[8,128]{1,0:T(8,128)} copy(f32[8,128]{1,0:T(8,128)} %shard_map.127) | data formatting | bytes 8192

commit v3 on v2

--- a/solution.py
+++ b/solution.py
@@ -64,7 +64,6 @@
     load_sem,
     ext,
     ifb,
-    ub,
     rows_out,
     rows_in,
     pick,
@@ -79,14 +78,42 @@
     rs_send,
     rs_recv,
 ):
-    n_patch, n_sub, nbd, gh, ig, erows, base, nbp, rbp = dims
+    n_patch, n_sub, nbd, gh, ig, erows, base, ifp, rbp = dims
     patch, sub = lax.axis_index("patch"), lax.axis_index("sub")
     upper = lax.rem(patch + 1, n_patch)
     lower = lax.rem(patch + n_patch - 1, n_patch)
-    peers = [lax.rem(sub + k, n_sub) for k in range(1, n_sub)]
+    steps = sorted(range(n_sub), key=lambda k: (abs(k - n_sub // 2), k))
+    has = (patch < n_patch - 1, patch > 0)
+    neighbours = jnp.where(has[0], n_sub, 0) + jnp.where(has[1], n_sub, 0)
+    peers = [lax.rem(sub + k, n_sub) for k in steps if k]
     sources = [lax.rem(sub + n_sub - k, n_sub) for k in range(1, n_sub)]
-    everyone = [lax.rem(sub + k, n_sub) for k in range(n_sub)]
-
+    everyone = [lax.rem(sub + k, n_sub) for k in steps]
+
+    far_rows = 2 * ig * n_sub
+    for side in range(2):
+        for s in range(n_sub):
+            for sweep in range(SWEEPS - 1):
+                ext[sweep, pl.ds(base + (side * n_sub + s) * 2 * ig + side * ig, ig), :] = (
+                    jnp.zeros((ig, 128), F32)
+                )
+
+        @pl.when(jnp.logical_not(has[1 - side]))
+        def clear():
+            for sweep in range(SWEEPS - 1):
+                ext[sweep, pl.ds(base + side * far_rows, far_rows), :] = jnp.zeros(
+                    (far_rows, 128), F32
+                )
+
+    barrier = pltpu.get_barrier_semaphore()
+    for side, other in ((0, upper), (1, lower)):
+
+        @pl.when(has[side])
+        def greet():
+            for peer in everyone:
+                pl.semaphore_signal(barrier, inc=1, device_id=(other, peer), device_id_type=MESH)
+
+    for peer in peers:
+        pl.semaphore_signal(barrier, inc=1, device_id=(patch, peer), device_id_type=MESH)
     pairs = (
         (residual_in, residual),
         (sends_in, sends),
@@ -107,12 +134,6 @@
     ]
     for load in loads:
         load.start()
-    barrier = pltpu.get_barrier_semaphore()
-    for peer in peers:
-        pl.semaphore_signal(barrier, inc=1, device_id=(patch, peer), device_id_type=MESH)
-    for other in (upper, lower):
-        for peer in everyone:
-            pl.semaphore_signal(barrier, inc=1, device_id=(other, peer), device_id_type=MESH)
 
     def solve(r):
         head, rest = halves(r)
@@ -125,46 +146,62 @@
             total = total + jnp.where(row == b, wide[:, b * 128 : (b + 1) * 128], 0.0)
         return total
 
+    def listed(scalars, rows):
+        row = lax.broadcasted_iota(jnp.int32, (rows, 128), 0)
+        index = jnp.full((rows, 128), -1, jnp.int32)
+        for i, scalar in enumerate(scalars):
+            index = jnp.where(row == i, scalar, index)
+        return index
+
+    def choose(u, index):
+        chosen = jnp.zeros(index.shape, F32)
+        for b in range(nbd):
+            chosen = jnp.where(index == b, u[b : b + 1], chosen)
+        return chosen
+
     def expand(u, sweep):
-        ub[sweep] = u
         first = pl.multiple_of(sub * erows, 8)
         ext[sweep, pl.ds(first, nbd), :] = u
-        for o in range(n_sub):
-            for j in range(gh):
-                ext[sweep, pl.ds(first + (nbd + o * gh + j), 1), :] = ub[
-                    sweep, pl.ds(sends[j, o], 1), :
-                ]
-        for side in range(2):
-            for j in range(ig):
-                ifb[sweep, pl.ds(side * ig + j, 1), :] = ub[sweep, pl.ds(ifaces[side, j], 1), :]
+        ext[sweep, pl.ds(first + nbd, erows - nbd), :] = choose(u, send_index)
+        ifb[sweep] = choose(u, iface_index)
+
+    def far_copies(sweep, side, other):
+        place = pl.ds(base + (side * n_sub + sub) * 2 * ig + (1 - side) * ig, ig)
+        listed_rows = pl.ds((1 - side) * ig, ig)
+        return [
+            pltpu.make_async_remote_copy(
+                src_ref=ifb.at[sweep, listed_rows],
+                dst_ref=ext.at[sweep, place],
+                send_sem=if_send.at[sweep, side, k],
+                recv_sem=if_recv.at[sweep, side, sub],
+                device_id=(other, peer),
+                device_id_type=MESH,
+            )
+            for k, peer in enumerate(everyone)
+        ]
+
+    def far_each(sweep, act):
+        for side, other in ((0, upper), (1, lower)):
+
+            @pl.when(has[side])
+            def run():
+                for copy in far_copies(sweep, side, other):
+                    act(copy)
 
     def spread(sweep):
-        copies = []
         mine = pl.ds(pl.multiple_of(sub * erows, 8), erows)
-        for side, other in ((0, upper), (1, lower)):
-            place = pl.ds(pl.multiple_of(base + (side * n_sub + sub) * 2 * ig, 8), 2 * ig)
-            for k, peer in enumerate(everyone):
-                copies.append(
-                    pltpu.make_async_remote_copy(
-                        src_ref=ifb.at[sweep],
-                        dst_ref=ext.at[sweep, place],
-                        send_sem=if_send.at[sweep, side, k],
-                        recv_sem=if_recv.at[sweep, side, sub],
-                        device_id=(other, peer),
-                        device_id_type=MESH,
-                    )
-                )
-        for k, peer in enumerate(peers):
-            copies.append(
-                pltpu.make_async_remote_copy(
-                    src_ref=ext.at[sweep, mine],
-                    dst_ref=ext.at[sweep, mine],
-                    send_sem=ag_send.at[sweep, k],
-                    recv_sem=ag_recv.at[sweep, sub],
-                    device_id=(patch, peer),
-                    device_id_type=MESH,
-                )
+        far_each(sweep, lambda copy: copy.start())
+        copies = [
+            pltpu.make_async_remote_copy(
+                src_ref=ext.at[sweep, mine],
+                dst_ref=ext.at[sweep, mine],
+                send_sem=ag_send.at[sweep, k],
+                recv_sem=ag_recv.at[sweep, sub],
+                device_id=(patch, peer),
+                device_id_type=MESH,
             )
+            for k, peer in enumerate(peers)
+        ]
         for copy in copies:
             copy.start()
         return copies
@@ -180,16 +217,33 @@
                 device_id=(patch, source),
                 device_id_type=MESH,
             ).wait_recv()
+
+    def gathered_far(sweep):
         for side in range(2):
-            for s in range(n_sub):
-                pltpu.make_async_remote_copy(
-                    src_ref=ifb.at[sweep],
-                    dst_ref=ext.at[sweep, pl.ds(base + (side * n_sub + s) * 2 * ig, 2 * ig)],
-                    send_sem=if_send.at[sweep, side, s],
-                    recv_sem=if_recv.at[sweep, side, s],
-                    device_id=(lower, s),
-                    device_id_type=MESH,
-                ).wait_recv()
+
+            @pl.when(has[1 - side])
+            def arrive():
+                for s in range(n_sub):
+                    pltpu.make_async_remote_copy(
+                        src_ref=ifb.at[sweep, pl.ds((1 - side) * ig, ig)],
+                        dst_ref=ext.at[sweep, pl.ds(base + (side * n_sub + s) * 2 * ig + (1 - side) * ig, ig)],
+                        send_sem=if_send.at[sweep, side, s],
+                        recv_sem=if_recv.at[sweep, side, s],
+                        device_id=(patch, s),
+                        device_id_type=MESH,
+                    ).wait_recv()
+
+    def segments(sweep, first, count):
+        flat = jnp.transpose(ext[sweep, pl.ds(first, count), :])
+        head, rest = halves(flat)
+        size = flat.shape[0] // 2
+        return jnp.concatenate(
+            [
+                jnp.concatenate([head[:size], head[size:]], axis=1),
+                jnp.concatenate([rest[:size], rest[size:]], axis=1),
+            ],
+            axis=0,
+        ).astype(BF16)
 
     for load in loads[:4]:
         load.wait()
@@ -198,13 +252,15 @@
     p_head = p_all.astype(BF16)
     ph[...] = p_head
     plo[...] = (p_all - p_head.astype(F32)).astype(BF16)
-    used = base + 4 * ig * n_sub
-    if nbp > used:
-        for sweep in range(SWEEPS - 1):
-            ext[sweep, pl.ds(used, nbp - used), :] = jnp.zeros((nbp - used, 128), F32)
+    for first, end in ((n_sub * erows, base), (base + 4 * ig * n_sub, base + ifp)):
+        if end > first:
+            for sweep in range(SWEEPS - 1):
+                ext[sweep, pl.ds(first, end - first), :] = jnp.zeros((end - first, 128), F32)
+    send_index = listed([sends[j, o] for o in range(n_sub) for j in range(gh)], erows - nbd)
+    iface_index = listed([ifaces[side, j] for side in range(2) for j in range(ig)], 2 * ig)
     u = solve(r)
     expand(u, 0)
-    pl.semaphore_wait(barrier, n_sub - 1 + 2 * n_sub)
+    pl.semaphore_wait(barrier, n_sub - 1 + neighbours)
     copies = spread(0)
 
     for load in loads[4:]:
@@ -234,14 +290,14 @@
     side = far >> log2(ig)
     own_place = o * erows + col
     near_place = (near >> log2(gh)) * erows + nbd + o * gh + (near & (gh - 1))
-    far_place = base + (side * n_sub + o) * 2 * ig + (1 - side) * ig + (far & (ig - 1))
+    far_place = 2 * base + (side * n_sub + o) * 2 * ig + (1 - side) * ig + (far & (ig - 1))
     neighbour = patch - 1 + 2 * side
-    far_place = jnp.where((neighbour >= 0) & (neighbour < n_patch), far_place, -2 * nbp)
+    far_place = jnp.where((neighbour >= 0) & (neighbour < n_patch), far_place, -4 * (base + ifp))
     place = jnp.where(near < 0, own_place, jnp.where(far < 0, near_place, far_place))
-    place = place + (quad & 1) * nbp
+    place = place + (quad & 1) * jnp.where(far < 0, base, ifp)
     active = lax.broadcasted_iota(jnp.int32, (1, elements), 1) < counts[...]
     target = jnp.where(active, block + (quad >> 1) * rbp, -1)
-    for i in range(2 * nbp // 128):
+    for i in range(2 * (base + ifp) // 128):
         index = lax.broadcasted_iota(jnp.int32, (128, elements), 0) + i * 128
         pick[pl.ds(i * 128, 128), :] = jnp.where(index == place, 1.0, 0.0).astype(BF16)
     for i in range(2 * rbp // 128):
@@ -250,16 +306,10 @@
 
     for sweep in range(SWEEPS - 1):
         gathered(sweep)
-        flat = jnp.transpose(ext[sweep])
-        head, rest = halves(flat)
-        segments = jnp.concatenate(
-            [
-                jnp.concatenate([head[:functions], head[functions:]], axis=1),
-                jnp.concatenate([rest[:functions], rest[functions:]], axis=1),
-            ],
-            axis=0,
-        ).astype(BF16)
-        x = dot(segments, pick[...]).astype(BF16)
+        x = dot(segments(sweep, 0, base), pick[pl.ds(0, 2 * base), :])
+        gathered_far(sweep)
+        x = x + dot(segments(sweep, base, ifp), pick[pl.ds(2 * base, 2 * ifp), :])
+        x = x.astype(BF16)
         gx = dot(left, jnp.concatenate([x, x], axis=0))
         vx = gx[3 * points :]
         k0 = terms[pl.ds(0, points), :]
@@ -287,6 +337,9 @@
             )
             copy.start()
             copies.append(copy)
+        for copy in copies:
+            copy.wait_send()
+        far_each(sweep, lambda copy: copy.wait_send())
         applied = mass[...] * u + rows_out[sweep, pl.ds(pl.multiple_of(sub * nbd, 8), nbd), :]
         for k, source in enumerate(sources):
             pltpu.make_async_remote_copy(
@@ -301,10 +354,8 @@
         u = u + solve(r - applied)
         if sweep < SWEEPS - 2:
             expand(u, sweep + 1)
-            copies += spread(sweep + 1)
+            copies = spread(sweep + 1)
     out[...] = u
-    for copy in copies:
-        copy.wait_send()
 
 
 def body(
@@ -328,10 +379,11 @@
     elements = element_temps.shape[0]
     quads = basis_values.shape[0]
     erows = -(-(nbd + n_sub * gh) // 8) * 8
-    base = n_sub * erows
-    nbp = -(-(base + 4 * ig * n_sub) // 128) * 128
+    base = -(-(n_sub * erows) // 128) * 128
+    ifp = -(-(4 * ig * n_sub) // 128) * 128
+    nbp = base + ifp
     rbp = -(-(n_sub * nbd) // 128) * 128
-    dims = (n_patch, n_sub, nbd, gh, ig, erows, base, nbp, rbp)
+    dims = (n_patch, n_sub, nbd, gh, ig, erows, base, ifp, rbp)
     steps = SWEEPS - 1
     vmem = pl.BlockSpec(memory_space=pltpu.VMEM)
     hbm = pl.BlockSpec(memory_space=pltpu.HBM)
@@ -358,7 +410,6 @@
             dma((13,)),
             pltpu.VMEM((steps, nbp, points), F32),
             pltpu.VMEM((steps, 2 * ig, points), F32),
-            pltpu.VMEM((steps, nbd, points), F32),
             pltpu.VMEM((steps, rbp, points), F32),
             pltpu.VMEM((steps, n_sub, nbd, points), F32),
             pltpu.VMEM((2 * nbp, elements), BF16),

time: 32 us -> 30.1 us (0.941)
  Pallas kernels: 29.9 us -> 27.9 us
    pallas_call x1, Pallas kernels: 29.9 us -> 27.9 us  [body(): pl.pallas_call(functools.partial(kernel, dims), out_shape=jax.ShapeDtypeS...]
where the time goes in v3:
time: 30.1 us; the launch traced here: 29.9 us
  Pallas kernels  27.9 us (93%)
  local copies, waits for them, and re-layouts  1.28 us (4%)
  between operations  0.66 us (2%)
    pallas_call x1, Pallas kernels, body(): pl.pallas_call(functools.partial(kernel, dims), out_shape=jax.ShapeDtypeS...  27.9 us
    unnamed x1, local copies, waits for them, and re-layouts  1.28 us

profile of v3, /device:TPU:0, one launch (start us, length us, event | category | flops | bytes accessed | tf_op | source)
XLA Modules:
  0.0 29.9 jit_solution(5713926773265369514)
XLA Ops:
  0.7 27.9 %shard_map.127 = f32[8,128]{1,0:T(8,128)} custom-call(f32[64,512]{1,0:T(8,128)} %bitcast.8, f32[64,512]{1,0:T(8,128)} %bitcast.9, f32[64,64]{1,0:T(8,128)} %values_in.1, f32[3,64,64]{2,1,0:T(8,128)} %grads_in.1, s32[1,512]{1,0:T(1,128)} %bitcast.10, s32[1,512]{1,0:T(1,128)} %bitcast.11, s32[1,512]{1,0:T(1,128)} %bitcast.12, s32[1,1]{1,0:T(1,128)} %bitcast.7.counts_in, ...), custom_call_target="tpu_custom_call" | custom-call | tf_op jit(solution)/shard_map/pallas_call | solution.py:391
  28.6 1.3 %copy.16 = f32[8,128]{1,0:T(8,128)} copy(f32[8,128]{1,0:T(8,128)} %shard_map.127) | data formatting | bytes 8192
